TPU v7x, 512 devices: a whole 4x4x16 slice. The times are simulated.
512 devices in a mesh: dp: 64 (over x_lo, z, core), fsdp: 8 (over y, x_hi).
Axes of the slice: x: 4 (x_hi: 2, x_lo: 2; x = x_hi * 2 + x_lo), y: 4, z: 16, core: 2. Of those that a mesh axis runs over, the one named last changes fastest.
Arguments:
- tokens: bfloat16 [65536, 1024], P('dp'), may hold values from -8 to 8
- teacher: bfloat16 [512, 6144], P('dp'), may hold values from -8 to 8
- norm_gain: float32 [1024], replicated, may hold values from 0.25 to 1.75
- w_in: bfloat16 [1024, 4096], P(None, 'fsdp'), may hold values from -0.1875 to 0.1875
- b_in: float32 [4096], P('fsdp'), may hold values from -3 to 3
- w_out: bfloat16 [1024, 4096], P(None, 'fsdp'), may hold values from -0.09375 to 0.09375
- b_out: float32 [1024], replicated, may hold values from -3 to 3
- final_gain: float32 [1024], replicated, may hold values from 0.25 to 1.75
Outputs:
- loss_value: float32 [], replicated
- grad_in: bfloat16 [1024, 4096], P('dp', 'fsdp')
- grad_out: bfloat16 [1024, 4096], P('dp', 'fsdp')
All inputs are finite; a program needn't handle non-finite values.
Results may differ from a plain program's by a relative error of at most 0.008.
Values may be sent and summed in bfloat16 or wider, within the bound.
A program may use at most 64 MiB of HBM per device.

v0:
```python
import jax
import jax.numpy as jnp
from jax import lax
from jax.sharding import PartitionSpec as P

loss_scale = 4096.0


def gelu_tanh(values):
    inner = 0.7978845608 * (values + 0.044715 * values * values * values)
    return 0.5 * values * (1.0 + jnp.tanh(inner))


def gelu_slope(values):
    inner = 0.7978845608 * (values + 0.044715 * values * values * values)
    tangent = jnp.tanh(inner)
    return 0.5 * (1.0 + tangent) + 0.5 * values * (1.0 - tangent * tangent) * 0.7978845608 * (
        1.0 + 3.0 * 0.044715 * values * values
    )


def layer_norm(values, gain_vec):
    centered = values - jnp.mean(values, axis=-1, keepdims=True)
    inv_std = lax.rsqrt(jnp.mean(centered * centered, axis=-1, keepdims=True) + 1e-05)
    normed = centered * inv_std
    return (normed * gain_vec, normed, inv_std)


def contract_last(left_side, right_side):
    return lax.dot_general(
        left_side, right_side, (((1,), (1,)), ((), ())), preferred_element_type=jnp.float32
    )


def contract_first(left_side, right_side):
    return lax.dot_general(
        left_side, right_side, (((0,), (0,)), ((), ())), preferred_element_type=jnp.float32
    )


def body(tokens, teacher, norm_gain, w_in, b_in, w_out, b_out, final_gain):
    dp_size = lax.axis_size("dp")
    fsdp_size = lax.axis_size("fsdp")
    block_rows = teacher.shape[0]
    model_width = tokens.shape[1]
    per_image = tokens.shape[0] // block_rows
    image_count = block_rows * dp_size
    token_values = tokens.astype(jnp.float32)
    normed_tokens = layer_norm(token_values, norm_gain)[0].astype(jnp.bfloat16)
    pre_act = jnp.dot(normed_tokens, w_in, preferred_element_type=jnp.float32) + b_in
    hidden = pre_act.shape[1]
    pooled = (
        gelu_tanh(pre_act).reshape(block_rows, per_image, hidden).mean(axis=1).astype(jnp.bfloat16)
    )
    token_mean = token_values.reshape(block_rows, per_image, model_width).mean(axis=1)
    partial_value = contract_last(pooled, w_out)
    embedding = token_mean + lax.psum(partial_value, "fsdp") + b_out
    scaled_unit, normed_embed, inv_std = layer_norm(embedding, final_gain)
    unit_norm = jnp.sqrt(jnp.sum(scaled_unit * scaled_unit, axis=-1, keepdims=True) + 1e-06)
    unit_dir = scaled_unit / unit_norm
    student = unit_dir.astype(jnp.bfloat16)
    teacher_f = teacher.astype(jnp.float32)
    target = (
        teacher_f / jnp.sqrt(jnp.sum(teacher_f * teacher_f, axis=-1, keepdims=True) + 1e-06)
    ).astype(jnp.bfloat16)
    rows_each = block_rows // fsdp_size
    first_row = lax.axis_index("fsdp") * rows_each
    own_student = lax.dynamic_slice_in_dim(student, first_row, rows_each, 0)
    own_target = lax.dynamic_slice_in_dim(target, first_row, rows_each, 0)
    piece_student = lax.all_gather(student, "dp", axis=0, tiled=True)
    piece_target = lax.all_gather(target, "dp", axis=0, tiled=True)
    resid = contract_last(own_student, piece_student) - contract_last(own_target, piece_target)
    grad_acc = jnp.dot(
        resid.astype(jnp.bfloat16), piece_student, preferred_element_type=jnp.float32
    )
    sum_part = jnp.sum(resid * resid)
    grad_sum = lax.all_gather(grad_acc, "fsdp", axis=0, tiled=True)
    loss_value = lax.psum(sum_part, ("dp", "fsdp")) / image_count
    dstudent = loss_scale * 4.0 / image_count * grad_sum
    dunit = (dstudent - unit_dir * jnp.sum(unit_dir * dstudent, axis=-1, keepdims=True)) / unit_norm
    gain_grad = dunit * final_gain
    dembed = inv_std * (
        gain_grad
        - jnp.mean(gain_grad, axis=-1, keepdims=True)
        - normed_embed * jnp.mean(gain_grad * normed_embed, axis=-1, keepdims=True)
    )
    dembed_b = dembed.astype(jnp.bfloat16)
    dpooled = jnp.dot(dembed_b, w_out, preferred_element_type=jnp.float32)
    slope = gelu_slope(pre_act.reshape(block_rows, per_image, hidden))
    dhidden = (
        (dpooled[:, None, :] / per_image * slope)
        .reshape(block_rows * per_image, hidden)
        .astype(jnp.bfloat16)
    )
    in_term = contract_first(normed_tokens, dhidden)
    out_term = contract_first(dembed_b, pooled)
    shares = lax.psum_scatter(
        jnp.concatenate([in_term, out_term], axis=1), "dp", scatter_dimension=0, tiled=True
    )
    grad_in = shares[:, :hidden].astype(jnp.bfloat16)
    grad_out = shares[:, hidden:].astype(jnp.bfloat16)
    return (loss_value, grad_in, grad_out)


def solution(mesh):
    return jax.shard_map(
        body,
        mesh=mesh,
        in_specs=(
            P("dp", None),
            P("dp", None),
            P(),
            P(None, "fsdp"),
            P("fsdp"),
            P(None, "fsdp"),
            P(),
            P(),
        ),
        out_specs=(P(), P("dp", "fsdp"), P("dp", "fsdp")),
        check_vma=False,
    )
```

profile of v0, /device:TPU:4, one launch (start us, length us, event | category | flops | bytes accessed | tf_op | source)
XLA Modules:
  0.0 595.0 jit_solution(14809419079678232370)
XLA Ops:
  7.2 2.1 convert_reduce_fusion
  9.3 0.2 copy-done.1
  9.5 0.4 bitcast_reduce_fusion
  9.9 0.7 multiply_reduce_fusion
  10.7 3.3 bitcast_reduce_fusion.1
  13.9 0.4 fusion.16
  14.3 40.4 %psum.14 = f32[8,1024]{1,0:T(8,128)S(1)} all-reduce(f32[8,1024]{1,0:T(8,128)S(1)} %fusion.16), channel_id=1, replica_groups=mesh['dp'=64,'fsdp'=8] {'fsdp'}, use_global_device_ids=true, to_apply=%region_4.0 | all-reduce | flops 8192 | bytes 65536 | tf_op jit(solution)/shard_map/psum | solution.py:57
  54.9 0.2 multiply_reduce_fusion.4
  55.1 0.2 multiply_reduce_fusion.3
  55.3 0.7 fusion.21
  56.1 0.2 fusion.7
  56.2 0.7 fusion.8
  57.0 120.5 %all-gather.4.cloned.1.call-done = bf16[512,1024]{1,0:T(8,128)(2,1)} async-done(((bf16[8,1024]{1,0:T(8,128)(2,1)}), bf16[512,1024]{1,0:T(8,128)(2,1)}) %all-gather.4.cloned.1.call-update) | async-done | bytes 1048592 | tf_op jit(solution)/shard_map/all_gather | solution.py:70
  177.5 1.6 fusion.12
  179.1 124.2 %all-gather.6.cloned.1.call-done = bf16[512,6144]{1,0:T(8,128)(2,1)} async-done(((bf16[8,6144]{1,0:T(8,128)(2,1)}), bf16[512,6144]{1,0:T(8,128)(2,1)}) %all-gather.6.cloned.1.call-update) | async-done | bytes 6291472 | tf_op jit(solution)/shard_map/all_gather | solution.py:71
  303.3 4.6 fusion.9
  308.0 0.6 subtract_convert_fusion
  308.6 0.2 fusion.27
  308.9 34.2 %all-gather = f32[8192]{0:T(1024)S(1)} all-gather(f32[1024]{0:T(1024)S(1)} %bitcast.24), channel_id=2, replica_groups=mesh['dp'=64,'fsdp'=8] {'fsdp'}, dimensions={0}, use_global_device_ids=true | all-gather | bytes 36864 | tf_op jit(solution)/shard_map/all_gather | solution.py:77
  343.1 0.2 multiply_reduce_fusion.2
  343.3 0.2 fusion.24
  343.5 1.7 convolution_multiply_fusion
  345.2 0.5 fusion.15
  345.7 1.4 fusion.6
  347.1 1.5 fusion.22
  348.6 2.5 pad_maximum_fusion
  351.1 5.3 copy.15
  356.5 99.2 %psum.15 = f32[]{:T(128)} all-reduce(f32[]{:T(128)} %get-tuple-element.17), channel_id=1, replica_groups=mesh['dp'=64,'fsdp'=8] {'dp','fsdp'}, use_global_device_ids=true, to_apply=%region_10.0 | all-reduce | flops 1 | bytes 8 | tf_op jit(solution)/shard_map/psum | solution.py:78
  456.4 128.5 %reduce-scatter.4.cloned.1.call-done = f32[16,1024]{1,0:T(8,128)} async-done(((f32[1024,1024]{1,0:T(8,128)}), f32[16,1024]{1,0:T(8,128)}) %reduce-scatter.4.cloned.1.call-update) | async-done | bytes 65552
  584.9 1.0 copy.16
  586.0 0.7 copy.14
  586.7 0.7 copy.13
  (37 shorter events, 0.4 us)
Async XLA Ops:
  7.2 3.4 copy-start
  7.2 2.3 copy-start.1
  7.2 170.3 %all-gather.4.cloned.1.call-start = ((), (), s32[]{:S(2)}) async-start(), calls=%async_computation.1 | async-start | bytes 1064960 | tf_op jit(solution)/shard_map/all_gather | solution.py:70
  9.5 1.1 copy-start.8
  9.5 1.1 copy-start.9
  10.6 3.3 copy-start.4
  10.6 44.1 %copy-start.7 = (f32[1024]{0:T(1024)S(1)}, f32[1024]{0:T(1024)}, u32[]{:S(2)}) copy-start(f32[1024]{0:T(1024)} %param.14) | copy-start | bytes 12292
  10.7 44.4 %copy-start.6 = (f32[1024]{0:T(1024)S(1)}, f32[1024]{0:T(1024)}, u32[]{:S(2)}) copy-start(f32[1024]{0:T(1024)} %param.15) | copy-start | bytes 12292
  10.7 45.4 %copy-start.5 = (bf16[8,6144]{1,0:T(8,128)(2,1)S(1)}, bf16[8,6144]{1,0:T(8,128)(2,1)}, u32[]{:S(2)}) copy-start(bf16[8,6144]{1,0:T(8,128)(2,1)} %param.9) | copy-start | bytes 294916
  56.0 247.3 %all-gather.6.cloned.1.call-start = ((), (), s32[]{:S(2)}) async-start(), calls=%async_computation.2 | async-start | bytes 6389760 | tf_op jit(solution)/shard_map/all_gather | solution.py:71
  57.0 527.9 %reduce-scatter.4.cloned.1.call-start = ((), (), s32[]{:S(2)}) async-start(), calls=%async_computation.3 | async-start | bytes 4259840
  303.3 5.3 copy-start.2
  343.1 2.6 copy-start.3
Sparse Core Ops, SparseCore 0:
  56.1 121.3 all-gather.3
  179.7 123.6 all-gather.5
  356.6 228.2 reduce-scatter.3
where the time goes:
time: 595 us
  waiting for transfers between devices  373 us (63%)
  blocking collectives  174 us (29%)
  between operations  15.7 us (3%)
  matrix products  13.8 us (2%)
  other arithmetic  10.2 us (2%)
  local copies, waits for them, and re-layouts  8 us (1%)
    unnamed x4, waiting for transfers between devices  129 us
    all_gather x1, waiting for transfers between devices, body(): piece_target = lax.all_gather(target, 'dp', axis=0, tiled=True)  124 us
    all_gather x1, waiting for transfers between devices, body(): piece_student = lax.all_gather(student, 'dp', axis=0, tiled=True)  120 us
    psum x1, blocking collectives, body(): loss_value = lax.psum(sum_part, ('dp', 'fsdp')) / image_count  99.2 us
    psum x1, blocking collectives, body(): embedding = token_mean + lax.psum(partial_value, 'fsdp') + b_out  40.4 us
    all_gather x1, blocking collectives, body(): grad_sum = lax.all_gather(grad_acc, 'fsdp', axis=0, tiled=True)  34.2 us
  transfers between devices with their start and end apart: 3, of which 3 were waited for; matrix products, arithmetic and copies ran while one was open for 0% of the time, Pallas kernels for 0%

commit v1 on v0

--- a/solution.py
+++ b/solution.py
@@ -54,7 +54,7 @@
     )
     token_mean = token_values.reshape(block_rows, per_image, model_width).mean(axis=1)
     partial_value = contract_last(pooled, w_out)
-    embedding = token_mean + lax.psum(partial_value, "fsdp") + b_out
+    embedding = token_mean + jnp.sum(lax.all_gather(partial_value, "fsdp"), 0) + b_out
     scaled_unit, normed_embed, inv_std = layer_norm(embedding, final_gain)
     unit_norm = jnp.sqrt(jnp.sum(scaled_unit * scaled_unit, axis=-1, keepdims=True) + 1e-06)
     unit_dir = scaled_unit / unit_norm

time: 595 us -> 593 us (level)
    psum x1 -> x0, blocking collectives: 40.4 us -> none  [body(): embedding = token_mean + lax.psum(partial_value, 'fsdp') + b_out]
    all_gather x0 -> x1, blocking collectives: none -> 35.3 us  [body(): lax.all_gather(partial_value, 'fsdp')]
where the time goes in v1:
time: 593 us
  waiting for transfers between devices  376 us (63%)
  blocking collectives  169 us (28%)
  between operations  15.7 us (3%)
  matrix products  13.8 us (2%)
  other arithmetic  10.2 us (2%)
  local copies, waits for them, and re-layouts  8 us (1%)
    unnamed x4, waiting for transfers between devices  129 us
    all_gather x1, waiting for transfers between devices, body(): piece_target = lax.all_gather(target, 'dp', axis=0, tiled=True)  124 us
    all_gather x1, waiting for transfers between devices, body(): piece_student = lax.all_gather(student, 'dp', axis=0, tiled=True)  123 us
    psum x1, blocking collectives, body(): loss_value = lax.psum(sum_part, ('dp', 'fsdp')) / image_count  99.3 us
    all_gather x1, blocking collectives, body(): lax.all_gather(partial_value, 'fsdp')  35.3 us
    all_gather x1, blocking collectives, body(): grad_sum = lax.all_gather(grad_acc, 'fsdp', axis=0, tiled=True)  34.2 us
  transfers between devices with their start and end apart: 3, of which 3 were waited for; matrix products, arithmetic and copies ran while one was open for 0% of the time, Pallas kernels for 0%

profile of v1, /device:TPU:4, one launch (start us, length us, event | category | flops | bytes accessed | tf_op | source)
XLA Modules:
  0.0 592.7 jit_solution(9736178518718344872)
XLA Ops:
  7.2 2.1 convert_reduce_fusion
  9.3 0.2 copy-done.1
  9.5 0.4 bitcast_reduce_fusion
  9.9 0.7 multiply_reduce_fusion
  10.7 3.3 bitcast_reduce_fusion.1
  13.9 0.4 fusion.16
  14.3 35.3 %all-gather = f32[64,1024]{1,0:T(8,128)S(1)} all-gather(f32[8,1024]{1,0:T(8,128)S(1)} %fusion.16), channel_id=2, replica_groups=mesh['dp'=64,'fsdp'=8] {'fsdp'}, dimensions={0}, use_global_device_ids=true | all-gather | bytes 294912 | tf_op jit(solution)/shard_map/all_gather | solution.py:57
  49.7 0.2 multiply_reduce_fusion.4
  49.9 0.2 multiply_reduce_fusion.3
  50.2 0.7 fusion.21
  50.9 0.2 fusion.7
  51.1 0.7 fusion.8
  51.9 123.3 %all-gather.5.cloned.1.call-done = bf16[512,1024]{1,0:T(8,128)(2,1)} async-done(((bf16[8,1024]{1,0:T(8,128)(2,1)}), bf16[512,1024]{1,0:T(8,128)(2,1)}) %all-gather.5.cloned.1.call-update) | async-done | bytes 1048592 | tf_op jit(solution)/shard_map/all_gather | solution.py:70
  175.2 1.6 fusion.12
  176.9 124.2 %all-gather.7.cloned.1.call-done = bf16[512,6144]{1,0:T(8,128)(2,1)} async-done(((bf16[8,6144]{1,0:T(8,128)(2,1)}), bf16[512,6144]{1,0:T(8,128)(2,1)}) %all-gather.7.cloned.1.call-update) | async-done | bytes 6291472 | tf_op jit(solution)/shard_map/all_gather | solution.py:71
  301.1 4.6 fusion.9
  305.7 0.6 subtract_convert_fusion
  306.3 0.2 fusion.27
  306.6 34.2 %all-gather.1 = f32[8192]{0:T(1024)S(1)} all-gather(f32[1024]{0:T(1024)S(1)} %bitcast.26), channel_id=3, replica_groups=mesh['dp'=64,'fsdp'=8] {'fsdp'}, dimensions={0}, use_global_device_ids=true | all-gather | bytes 36864 | tf_op jit(solution)/shard_map/all_gather | solution.py:77
  340.8 0.2 multiply_reduce_fusion.2
  341.0 0.2 fusion.24
  341.2 1.7 convolution_multiply_fusion
  343.0 0.5 fusion.15
  343.5 1.4 fusion.6
  344.9 1.5 fusion.22
  346.3 2.5 pad_maximum_fusion
  348.8 5.3 copy.17
  354.2 99.3 %psum.7 = f32[]{:T(128)} all-reduce(f32[]{:T(128)} %get-tuple-element.20), channel_id=1, replica_groups=mesh['dp'=64,'fsdp'=8] {'dp','fsdp'}, use_global_device_ids=true, to_apply=%region_10.0 | all-reduce | flops 1 | bytes 8 | tf_op jit(solution)/shard_map/psum | solution.py:78
  454.2 128.5 %reduce-scatter.4.cloned.1.call-done = f32[16,1024]{1,0:T(8,128)} async-done(((f32[1024,1024]{1,0:T(8,128)}), f32[16,1024]{1,0:T(8,128)}) %reduce-scatter.4.cloned.1.call-update) | async-done | bytes 65552
  582.7 1.0 copy.18
  583.7 0.7 copy.16
  584.4 0.7 copy.15
  (38 shorter events, 0.5 us)
Async XLA Ops:
  7.2 3.4 copy-start
  7.2 2.3 copy-start.1
  7.2 168.1 %all-gather.5.cloned.1.call-start = ((), (), s32[]{:S(2)}) async-start(), calls=%async_computation.1 | async-start | bytes 1064960 | tf_op jit(solution)/shard_map/all_gather | solution.py:70
  9.5 1.1 copy-start.8
  9.5 1.1 copy-start.9
  10.6 3.3 copy-start.4
  10.6 39.0 %copy-start.7 = (f32[1024]{0:T(1024)S(1)}, f32[1024]{0:T(1024)}, u32[]{:S(2)}) copy-start(f32[1024]{0:T(1024)} %param.14) | copy-start | bytes 12292
  10.7 39.3 %copy-start.6 = (f32[1024]{0:T(1024)S(1)}, f32[1024]{0:T(1024)}, u32[]{:S(2)}) copy-start(f32[1024]{0:T(1024)} %param.15) | copy-start | bytes 12292
  10.7 40.3 %copy-start.5 = (bf16[8,6144]{1,0:T(8,128)(2,1)S(1)}, bf16[8,6144]{1,0:T(8,128)(2,1)}, u32[]{:S(2)}) copy-start(bf16[8,6144]{1,0:T(8,128)(2,1)} %param.9) | copy-start | bytes 294916
  50.9 250.2 %all-gather.7.cloned.1.call-start = ((), (), s32[]{:S(2)}) async-start(), calls=%async_computation.2 | async-start | bytes 6389760 | tf_op jit(solution)/shard_map/all_gather | solution.py:71
  51.9 530.8 %reduce-scatter.4.cloned.1.call-start = ((), (), s32[]{:S(2)}) async-start(), calls=%async_computation.3 | async-start | bytes 4259840
  301.1 5.3 copy-start.2
  340.8 2.6 copy-start.3
Sparse Core Ops, SparseCore 0:
  51.0 124.2 all-gather.4
  177.4 123.6 all-gather.6
  354.3 228.2 reduce-scatter.3
